TPU v7x, 32 devices: a whole 2x2x4 slice. The times are simulated.
32 devices in a mesh: group: 2 (over y), expert: 4 (over z), tensor: 4 (over x, core).
Axes of the slice: x: 2, y: 2, z: 4, core: 2. Of those that a mesh axis runs over, the one named last changes fastest.
Arguments:
- q_absorbed: bfloat16 [1024, 36864], P(('group', 'expert'), 'tensor'), parts along dimension 0, may hold values from -14 to 14
- kv_latent: bfloat16 [1024, 576], P(('group', 'expert')), parts along dimension 0, may hold values from -4 to 4
- w_values: bfloat16 [64, 512, 128], P('tensor'), may hold values from -1 to 1
- w_out: bfloat16 [8192, 7168], P('tensor', 'expert'), may hold values from -0.0625 to 0.0625
- layer_input: bfloat16 [1024, 7168], P(('group', 'expert')), parts along dimension 0, may hold values from -40 to 40
- norm_gain: float32 [7168], replicated, may hold values from 0.1 to 1.9
- predicted: int32 [1024, 8], P(('group', 'expert')), parts along dimension 0, may hold values from 0 to 15, as said below
- actual: int32 [1024, 8], P(('group', 'expert')), parts along dimension 0, may hold values from 0 to 15, as said below
- gates: float32 [1024, 8], P(('group', 'expert')), parts along dimension 0, may hold values from 0.1 to 1
- w_gate: bfloat16 [16, 7168, 1024], P('expert', 'tensor'), may hold values from -0.0625 to 0.0625
- w_up: bfloat16 [16, 7168, 1024], P('expert', 'tensor'), may hold values from -0.0625 to 0.0625
- w_down: bfloat16 [16, 1024, 7168], P('expert', None, 'tensor'), may hold values from -0.1875 to 0.1875
Outputs:
- attended: bfloat16 [1024, 7168], P(('group', 'expert'), 'tensor'), parts along dimension 0
- mixture: bfloat16 [1024, 7168], P(('group', 'expert'), 'tensor'), parts along dimension 0
- missed: float32 [1024], P(('group', 'expert')), parts along dimension 0
There are 2 independent parts, one for each index of `group`. A program takes and returns all parts, laid end to end along the dimension named above; an argument that names none is the same for every part. Nothing has to cross between parts.
Inputs may be any that keep to these rules, and one draw needn't show every extreme that they name: `predicted`: each row names 8 different experts. In each aligned block of 128 rows (the rows of one index of expert) at most 80 rows name the same expert, and in every draw some expert is named by exactly 80 rows of every block. `actual`: each row names 8 different experts. In each aligned block of 128 rows (the rows of one index of expert) at most 12 rows name a given expert that the same row of predicted does not name, and in every draw some expert reaches 12 such rows in every block.
All inputs are finite; a program needn't handle non-finite values.
Results may differ from a plain program's by a relative error of at most 0.023.
Values may be sent and summed in bfloat16 or wider, within the bound.
A program may use at most 128 MiB of HBM per device.

v0:
```python
import functools

import jax
import jax.numpy as jnp
from jax import lax
from jax.experimental import pallas as pl
from jax.experimental.pallas import tpu as pltpu
from jax.sharding import PartitionSpec as P

ROPE = 64
VDIM = 128
CAP = 80
CAP_C = 12


EPS = 1e-06
FLOOR = -1e30


def bits_of(count):
    return count.bit_length() - 1


def share_of(index, count):
    share = 0
    for bit in range(bits_of(count)):
        share = share * 2 + ((index >> bit) & 1)
    return share


def halve(part, dim, bit, count):
    own = (lax.axis_index("tensor") >> bit) & 1
    half = part.shape[dim] // 2
    send = lax.dynamic_slice_in_dim(part, (1 - own) * half, half, dim).astype(jnp.bfloat16)
    keep = lax.dynamic_slice_in_dim(part, own * half, half, dim).astype(jnp.float32)
    got = lax.ppermute(send, "tensor", [(i, i ^ (1 << bit)) for i in range(count)])
    return keep + got.astype(jnp.float32)


def reduce_halving(part, dim, count):
    for bit in range(bits_of(count)):
        part = halve(part, dim, bit, count)
    return part


def gather_doubling(part, dim, count):
    for bit in reversed(range(bits_of(count))):
        own = (lax.axis_index("tensor") >> bit) & 1
        got = lax.ppermute(part, "tensor", [(i, i ^ (1 << bit)) for i in range(count)])
        first = jnp.where(own == 0, part, got)
        second = jnp.where(own == 0, got, part)
        part = jnp.concatenate([first, second], axis=dim)
    return part


def place_rows(gate, depth):
    tokens = gate.shape[1]
    chosen = gate > 0.0
    order = jnp.arange(tokens, dtype=jnp.int32)
    upper = (order[:, None] <= order[None, :]).astype(jnp.bfloat16)
    place = jnp.dot(chosen.astype(jnp.bfloat16), upper, preferred_element_type=jnp.float32)
    place = jnp.where(chosen, place.astype(jnp.int32) - 1, -1)
    row_ids = jnp.arange(depth, dtype=jnp.int32)
    picks = place[:, None, :] == row_ids[None, :, None]
    row_gate = jnp.sum(jnp.where(picks, gate[:, None, :], 0.0), axis=2)
    return picks.astype(jnp.bfloat16), row_gate


def attention(q_absorbed, kv_all, w_values):
    token_count = q_absorbed.shape[0]
    heads_here = w_values.shape[0]
    latent_width = w_values.shape[1]
    key_width = kv_all.shape[1]
    scale = (VDIM + ROPE) ** (-0.5)
    queries = q_absorbed.reshape(token_count * heads_here, key_width)
    query_pos = jnp.repeat(
        lax.axis_index("expert") * token_count + jnp.arange(token_count, dtype=jnp.int32),
        heads_here,
    )
    scores = (
        lax.dot_general(
            queries, kv_all, (((1,), (1,)), ((), ())), preferred_element_type=jnp.float32
        )
        * scale
    )
    key_pos = jnp.arange(kv_all.shape[0], dtype=jnp.int32)
    visible = query_pos[:, None] >= key_pos[None, :]
    masked = jnp.where(visible, scores, FLOOR)
    largest = jnp.max(masked, axis=1)
    expo = jnp.where(visible, jnp.exp(masked - largest[:, None]), 0.0)
    denominator = jnp.sum(expo, axis=1)
    accum = jnp.dot(
        expo.astype(jnp.bfloat16), kv_all[:, :latent_width], preferred_element_type=jnp.float32
    )
    latent = (
        (accum / denominator[:, None])
        .astype(jnp.bfloat16)
        .reshape(token_count, heads_here, latent_width)
    )
    heads_out = jnp.einsum(
        "thc,hcv->thv", latent, w_values, preferred_element_type=jnp.float32
    ).astype(jnp.bfloat16)
    return heads_out.reshape(token_count, heads_here * w_values.shape[2])

MESH = pl.DeviceIdType.MESH


def fused_kernel(
    picks_ref,
    picks_t_ref,
    row_gate_ref,
    normed_ref,
    heads_ref,
    w_gate_ref,
    w_up_ref,
    w_down_ref,
    w_out_ref,
    attended_ref,
    mixture_ref,
    gate_buf,
    up_buf,
    down_buf,
    out_buf,
    rows,
    for_core,
    own_half,
    from_core,
    for_x,
    own_quarter,
    from_x,
    act,
    total,
    mix_out,
    mix_in,
    heads,
    cols_part,
    cols_core,
    cols_for_x,
    cols_from_x,
    cols_out,
    cols_in,
    weight_sem,
    down_sem,
    out_sem,
    core_send,
    core_recv,
    x_send,
    x_recv,
    act_x_send,
    act_x_recv,
    act_core_send,
    act_core_recv,
    mix_send,
    mix_recv,
    heads_send,
    heads_recv,
    cols_send,
    cols_recv,
):
    steps = picks_ref.shape[0]
    local = w_gate_ref.shape[0]
    blocks, token_count, _ = heads.shape
    quarter = own_quarter.shape[3]
    width = normed_ref.shape[1]
    tile = 256
    z = lax.axis_index("expert")
    me = lax.axis_index("tensor")
    core = lax.rem(me, 2)
    side = me // 2
    core_peer = side * 2 + 1 - core
    x_peer = (1 - side) * 2 + core
    mine = core * 2 + side
    stays = (mine == z) & (z == me)

    def remote(src, dst, send, recv, peer):
        return pltpu.make_async_remote_copy(
            src_ref=src,
            dst_ref=dst,
            send_sem=send,
            recv_sem=recv,
            device_id=peer,
            device_id_type=MESH,
        )

    def weight_copies(s):
        slot, e = lax.rem(s, 2), lax.rem(s, local)
        return (
            pltpu.make_async_copy(w_gate_ref.at[e], gate_buf.at[slot], weight_sem.at[0, slot]),
            pltpu.make_async_copy(w_up_ref.at[e], up_buf.at[slot], weight_sem.at[1, slot]),
        )

    def down_copy(s):
        slot, e = lax.rem(s, 2), lax.rem(s, local)
        return pltpu.make_async_copy(w_down_ref.at[e], down_buf.at[slot], down_sem.at[slot])

    def out_copy(j):
        slot = lax.rem(j, 2)
        cols = pl.ds(pl.multiple_of(j * tile, tile), tile)
        return pltpu.make_async_copy(w_out_ref.at[:, cols], out_buf.at[slot], out_sem.at[slot])

    def core_copy(s):
        return remote(
            for_core.at[lax.rem(s, 2)],
            from_core.at[s],
            core_send.at[s],
            core_recv.at[s],
            {"tensor": core_peer},
        )

    def x_copy(s):
        return remote(
            for_x.at[lax.rem(s, 2)], from_x.at[s], x_send.at[s], x_recv.at[s], {"tensor": x_peer}
        )

    def act_x_copy(s):
        part = act.at[s, mine]
        return remote(part, part, act_x_send.at[s], act_x_recv.at[s], {"tensor": x_peer})

    def act_core_copy(s):
        part = act.at[s, pl.ds(core * 2, 2)]
        return remote(part, part, act_core_send.at[s], act_core_recv.at[s], {"tensor": core_peer})

    def heads_copy(k):
        peer = lax.rem(z + k, blocks)
        return remote(
            heads_ref, heads.at[z], heads_send.at[k - 1], heads_recv.at[z], {"expert": peer}
        )

    def heads_arrival(k):
        source = lax.rem(z + k, blocks)
        return remote(
            heads_ref, heads.at[source], heads_send.at[k - 1], heads_recv.at[source], {"expert": source}
        )

    def cols_core_copy():
        return remote(
            cols_part.at[pl.ds((1 - core) * 2, 2)],
            cols_core,
            cols_send.at[0],
            cols_recv.at[0],
            {"tensor": core_peer},
        )

    def cols_x_copy():
        return remote(
            cols_for_x, cols_from_x, cols_send.at[1], cols_recv.at[1], {"tensor": x_peer}
        )

    def cols_final_copy():
        return remote(
            cols_out,
            cols_in,
            cols_send.at[2],
            cols_recv.at[2],
            {"expert": mine, "tensor": z},
        )

    def mix_target(half, i):
        return half + i * (blocks - 1 - 2 * half)

    def mix_copy(half, i):
        return remote(
            mix_out.at[half, i],
            mix_in.at[z],
            mix_send.at[half, i],
            mix_recv.at[z],
            {"expert": mix_target(half, i)},
        )

    def mix_arrival(source):
        return remote(
            mix_out.at[0, 0],
            mix_in.at[source],
            mix_send.at[0, 0],
            mix_recv.at[source],
            {"expert": source},
        )

    for copy in weight_copies(0):
        copy.start()
    down_copy(0).start()
    barrier = pltpu.get_barrier_semaphore()

    def greet(peer):
        pl.semaphore_signal(barrier, inc=1, device_id=peer, device_id_type=MESH)

    greet({"tensor": core_peer})
    greet({"tensor": x_peer})
    for k in range(1, blocks):
        greet({"expert": lax.rem(z + k, blocks)})

    @pl.when(jnp.logical_not(stays))
    def _():
        greet({"expert": mine, "tensor": z})
        greet({"expert": me, "tensor": lax.rem(z, 2) * 2 + z // 2})

    @pl.when(stays)
    def _():
        pl.semaphore_wait(barrier, 1 + blocks)

    @pl.when(jnp.logical_not(stays))
    def _():
        pl.semaphore_wait(barrier, 3 + blocks)

    for k in range(1, blocks):
        heads_copy(k).start()
    heads[z] = heads_ref[...]

    def multiply(s):
        slot = lax.rem(s, 2)
        half_tokens = picks_ref.shape[2]
        first_token = pl.multiple_of(s // local * half_tokens, half_tokens)

        @pl.when(s + 1 < steps)
        def _():
            for copy in weight_copies(s + 1):
                copy.start()

        @pl.loop(0, width // tile)
        def _(j):
            cols = pl.ds(pl.multiple_of(j * tile, tile), tile)
            rows[:, cols] = jnp.dot(
                picks_ref[s],
                normed_ref[pl.ds(first_token, half_tokens), cols],
                preferred_element_type=jnp.float32,
            ).astype(jnp.bfloat16)

        for copy in weight_copies(s):
            copy.wait()
        for half, target in ((1 - core, for_core), (core, own_half)):
            for k, x_half in enumerate((1 - side, side)):
                first = pl.multiple_of((half * 2 + x_half) * quarter, quarter)
                cols = pl.ds(first, quarter)
                for m, buf in enumerate((gate_buf, up_buf)):
                    target[slot, 2 * k + m] = jnp.dot(
                        rows[...], buf[slot, :, cols], preferred_element_type=jnp.float32
                    ).astype(jnp.bfloat16)
            if target is for_core:
                core_copy(s).start()

    def add_core(s):
        slot = lax.rem(s, 2)
        core_copy(s).wait()
        for k in range(2):
            for_x[slot, k] = (
                own_half[slot, k].astype(jnp.float32) + from_core[s, k].astype(jnp.float32)
            ).astype(jnp.bfloat16)
        x_copy(s).start()
        for k in range(2):
            own_quarter[slot, k] = own_half[slot, 2 + k].astype(jnp.float32) + from_core[
                s, 2 + k
            ].astype(jnp.float32)

    def activate(s):
        slot = lax.rem(s, 2)
        x_copy(s).wait()
        gate = own_quarter[slot, 0] + from_x[s, 0].astype(jnp.float32)
        up = own_quarter[slot, 1] + from_x[s, 1].astype(jnp.float32)
        act[s, mine] = (gate / (1.0 + jnp.exp(-gate)) * up).astype(jnp.bfloat16)
        act_x_copy(s).start()

    def pass_on(s):
        act_x_copy(s).wait()
        act_core_copy(s).start()

    def project(s):
        slot = lax.rem(s, 2)

        @pl.when(s + 1 < steps)
        def _():
            down_copy(s + 1).start()

        @pl.when(lax.rem(s, local) == 0)
        def _():
            total[...] = jnp.zeros_like(total)

        act_core_copy(s).wait()
        down_copy(s).wait()

        @pl.loop(0, width // tile)
        def _(j):
            cols = pl.ds(pl.multiple_of(j * tile, tile), tile)
            out = jnp.zeros((act.shape[2], tile), jnp.float32)
            for q in range(act.shape[1]):
                out += jnp.dot(
                    act[s, q],
                    down_buf[slot, q * quarter : (q + 1) * quarter, cols],
                    preferred_element_type=jnp.float32,
                )
            out = (out * row_gate_ref[s]).astype(jnp.bfloat16)
            total[:, cols] += jnp.dot(picks_t_ref[s], out, preferred_element_type=jnp.float32)

        @pl.when(lax.rem(s, local) == local - 1)
        def _():
            half = s // local
            for i in range(2):
                mix_out[half, i] = total[i * token_count : (i + 1) * token_count, :].astype(
                    jnp.bfloat16
                )

                @pl.when(mix_target(half, i) != z)
                def _():
                    mix_copy(half, i).start()

                @pl.when(mix_target(half, i) == z)
                def _():
                    mix_in[z] = mix_out[half, i]

    def multiply_heads():
        out_copy(0).start()
        for k in range(1, blocks):
            heads_copy(k).wait_send()
            heads_arrival(k).wait_recv()

        @pl.loop(0, width // tile)
        def _(j):
            @pl.when(j + 1 < width // tile)
            def _():
                out_copy(j + 1).start()

            out_copy(j).wait()
            cols = pl.ds(pl.multiple_of(j * tile, tile), tile)
            for b in range(blocks // 2):
                part = heads[2 * b : 2 * b + 2].reshape(2 * token_count, heads.shape[2])
                part = jnp.dot(
                    part, out_buf[lax.rem(j, 2)], preferred_element_type=jnp.float32
                ).astype(jnp.bfloat16)
                cols_part[2 * b : 2 * b + 2, :, cols] = part.reshape(2, token_count, tile)

        cols_core_copy().start()

    def add_cols_core():
        cols_core_copy().wait()
        cols_for_x[...] = (
            cols_part[core * 2 + 1 - side].astype(jnp.float32)
            + cols_core[1 - side].astype(jnp.float32)
        ).astype(jnp.bfloat16)
        cols_x_copy().start()

    def add_cols_x():
        cols_x_copy().wait()
        cols_out[...] = (
            cols_part[mine].astype(jnp.float32)
            + cols_core[side].astype(jnp.float32)
            + cols_from_x[...].astype(jnp.float32)
        ).astype(jnp.bfloat16)

        @pl.when(jnp.logical_not(stays))
        def _():
            cols_final_copy().start()

    @pl.loop(0, steps + 4)
    def _(step):
        @pl.when((step >= 1) & (step < steps + 1))
        def _():
            add_core(step - 1)

        @pl.when(step < steps)
        def _():
            multiply(step)

        @pl.when((step >= 2) & (step < steps + 2))
        def _():
            activate(step - 2)

        @pl.when((step >= 3) & (step < steps + 3))
        def _():
            pass_on(step - 3)

        @pl.when(step >= 4)
        def _():
            project(step - 4)

        @pl.when(step == steps - 2)
        def _():
            multiply_heads()

        @pl.when(step == steps - 1)
        def _():
            add_cols_core()

        @pl.when(step == steps)
        def _():
            add_cols_x()

    @pl.when(jnp.logical_not(stays))
    def _():
        cols_final_copy().wait()
        attended_ref[...] = cols_in[...]

    @pl.when(stays)
    def _():
        attended_ref[...] = cols_out[...]

    for half in range(2):
        for i in range(2):

            @pl.when(mix_target(half, i) != z)
            def _():
                mix_copy(half, i).wait_send()

    for source in range(blocks):

        @pl.when(z != source)
        def _():
            mix_arrival(source).wait_recv()

    mixed = mix_in[0].astype(jnp.float32)
    for source in range(1, blocks):
        mixed += mix_in[source].astype(jnp.float32)
    mixture_ref[...] = mixed.astype(jnp.bfloat16)


def run_fused(picks, picks_t, row_gate, normed_all, heads_out, w_gate, w_up, w_down, w_out):
    steps, depth, half_tokens = picks.shape
    local, width, hidden = w_gate.shape
    token_count, head_width = heads_out.shape
    blocks = 4
    quarter = hidden // 4
    bf16, f32 = jnp.bfloat16, jnp.float32
    dma = pltpu.SemaphoreType.DMA
    vmem = pl.BlockSpec(memory_space=pltpu.VMEM)
    hbm = pl.BlockSpec(memory_space=pl.ANY)
    block = (token_count, width)
    return pl.pallas_call(
        fused_kernel,
        out_shape=[jax.ShapeDtypeStruct(block, bf16)] * 2,
        in_specs=[vmem] * 5 + [hbm] * 4,
        out_specs=[vmem] * 2,
        scratch_shapes=[
            pltpu.VMEM((2, width, hidden), bf16),
            pltpu.VMEM((2, width, hidden), bf16),
            pltpu.VMEM((2, hidden, width), bf16),
            pltpu.VMEM((2, head_width, 256), bf16),
            pltpu.VMEM((depth, width), bf16),
            pltpu.VMEM((2, 4, depth, quarter), bf16),
            pltpu.VMEM((2, 4, depth, quarter), bf16),
            pltpu.VMEM((steps, 4, depth, quarter), bf16),
            pltpu.VMEM((2, 2, depth, quarter), bf16),
            pltpu.VMEM((2, 2, depth, quarter), f32),
            pltpu.VMEM((steps, 2, depth, quarter), bf16),
            pltpu.VMEM((steps, 4, depth, quarter), bf16),
            pltpu.VMEM((half_tokens, width), f32),
            pltpu.VMEM((2, 2, *block), bf16),
            pltpu.VMEM((blocks, *block), bf16),
            pltpu.VMEM((blocks, token_count, head_width), bf16),
            pltpu.VMEM((blocks, *block), bf16),
            pltpu.VMEM((2, *block), bf16),
            pltpu.VMEM(block, bf16),
            pltpu.VMEM(block, bf16),
            pltpu.VMEM(block, bf16),
            pltpu.VMEM(block, bf16),
            dma((2, 2)),
            dma((2,)),
            dma((2,)),
        ]
        + [dma((steps,))] * 8
        + [dma((2, 2)), dma((blocks,)), dma((blocks - 1,)), dma((blocks,)), dma((3,)), dma((3,))],
        compiler_params=pltpu.CompilerParams(
            collective_id=0, has_side_effects=True, vmem_limit_bytes=60 * 1024 * 1024
        ),
        cost_estimate=pl.CostEstimate(
            flops=2 * steps * depth * width * (3 * hidden + 2 * half_tokens),
            bytes_accessed=6 * local * width * hidden * 2,
            transcendentals=steps * depth * quarter,
        ),
    )(picks, picks_t, row_gate, normed_all, heads_out, w_gate, w_up, w_down, w_out)


def body(
    n_expert,
    n_tensor,
    q_absorbed,
    kv_latent,
    w_values,
    w_out,
    layer_input,
    norm_gain,
    predicted,
    actual,
    gates,
    w_gate,
    w_up,
    w_down,
):
    local, slice_width, hidden = w_gate.shape
    experts = local * n_expert
    paired = n_tensor & (n_tensor - 1) == 0

    matches = predicted[:, None, :] == actual[:, :, None]
    matched = jnp.any(matches, axis=2)
    missed = jnp.sum(jnp.where(matched, 0.0, gates), axis=1)
    names = jnp.arange(experts, dtype=jnp.int32)
    gate_map = jnp.sum(
        jnp.where(actual[:, :, None] == names[None, None, :], gates[:, :, None], 0.0), axis=1
    )
    gate_terms, rest = [], gate_map
    for _ in range(3):
        term = lax.reduce_precision(rest, 8, 7)
        gate_terms.append(term.astype(jnp.bfloat16))
        rest = rest - term
    fill = -(kv_latent.shape[1] + 3 * experts) % 128
    gate_terms.append(jnp.zeros((gate_map.shape[0], fill), jnp.bfloat16))
    mixed = lax.all_gather(
        jnp.concatenate([kv_latent, *gate_terms], axis=1), "expert", axis=0, tiled=True
    )
    key_width = kv_latent.shape[1]
    kv_all = mixed[:, :key_width]
    gate_all = sum(
        mixed[:, key_width + i * experts : key_width + (i + 1) * experts].astype(jnp.float32)
        for i in range(3)
    )

    first_col = lax.axis_index("tensor") * slice_width
    features = layer_input.astype(jnp.float32)
    inverse = lax.rsqrt(jnp.mean(features * features, axis=1, keepdims=True) + EPS)
    mine = lax.dynamic_slice_in_dim(layer_input, first_col, slice_width, 1).astype(jnp.float32)
    gain_mine = lax.dynamic_slice_in_dim(norm_gain, first_col, slice_width, 0)
    normed = (mine * inverse * gain_mine).astype(jnp.bfloat16)
    normed_all = lax.all_gather(normed, "expert", axis=0, tiled=True)

    heads_out = attention(q_absorbed, kv_all, w_values)
    tokens = normed_all.shape[0]
    gate_here = lax.dynamic_slice_in_dim(
        gate_all, lax.axis_index("expert") * local, local, 1
    )
    if n_tensor == 4 and n_expert == 4 and hidden % 1024 == 0 and slice_width % 256 == 0:
        block = tokens // 4
        halves = [
            jnp.concatenate([part[:block], part[3 * block :], part[block : 3 * block]], axis=0)
            for part in (gate_here, normed_all)
        ]
        gate_halves = halves[0].reshape(2, 2 * block, local).transpose(0, 2, 1)
        depth = -(-2 * (CAP + CAP_C) // 16) * 16
        picks, row_gate = place_rows(gate_halves.reshape(2 * local, 2 * block), depth)
        attended, mixture = run_fused(
            picks,
            picks.transpose(0, 2, 1),
            row_gate[:, :, None],
            halves[1],
            heads_out,
            w_gate,
            w_up,
            w_down,
            w_out,
        )
        return (attended, mixture, missed)

    depth = n_expert * (CAP + CAP_C)
    picks, row_gate = place_rows(gate_here.T, depth)
    heads_all = lax.all_gather(heads_out, "expert", axis=0, tiled=True)
    outs = []
    for e in range(local):
        rows = jnp.dot(picks[e], normed_all, preferred_element_type=jnp.float32).astype(
            jnp.bfloat16
        )
        gate_part = jnp.dot(rows, w_gate[e], preferred_element_type=jnp.float32)
        up_part = jnp.dot(rows, w_up[e], preferred_element_type=jnp.float32)
        gate_part, up_part = gate_part.astype(jnp.bfloat16), up_part.astype(jnp.bfloat16)
        if paired:
            gate_share = reduce_halving(gate_part, 1, n_tensor)
            up_share = reduce_halving(up_part, 1, n_tensor)
        else:
            gate_share = lax.psum_scatter(gate_part, "tensor", scatter_dimension=1, tiled=True)
            up_share = lax.psum_scatter(up_part, "tensor", scatter_dimension=1, tiled=True)
            gate_share = gate_share.astype(jnp.float32)
            up_share = up_share.astype(jnp.float32)
        act_part = (jax.nn.silu(gate_share) * up_share).astype(jnp.bfloat16)
        if paired:
            act = gather_doubling(act_part, 1, n_tensor)
        else:
            act = lax.all_gather(act_part, "tensor", axis=1, tiled=True)
        out = jnp.dot(act, w_down[e], preferred_element_type=jnp.float32)
        outs.append((out * row_gate[e][:, None]).astype(jnp.bfloat16))
    partial_mix = lax.dot_general(
        picks.reshape(local * depth, tokens),
        jnp.concatenate(outs, axis=0),
        (((0,), (0,)), ((), ())),
        preferred_element_type=jnp.float32,
    ).astype(jnp.bfloat16)
    mixture = lax.psum_scatter(partial_mix, "expert", scatter_dimension=0, tiled=True)

    partial_cols = jnp.dot(heads_all, w_out, preferred_element_type=jnp.float32).astype(
        jnp.bfloat16
    )
    if paired and n_expert == n_tensor:
        summed = reduce_halving(partial_cols, 0, n_tensor).astype(jnp.bfloat16)
        attended = lax.ppermute(
            summed,
            ("expert", "tensor"),
            [
                (e * n_tensor + t, share_of(t, n_tensor) * n_tensor + e)
                for e in range(n_expert)
                for t in range(n_tensor)
            ],
        )
    else:
        partial_rows = lax.all_to_all(
            partial_cols, "expert", split_axis=0, concat_axis=1, tiled=True
        )
        attended = lax.psum_scatter(partial_rows, "tensor", scatter_dimension=1, tiled=True)
    return (attended, mixture, missed)


def solution(mesh):
    placed = (
        P(("group", "expert"), "tensor"),
        P(("group", "expert"), None),
        P("tensor", None, None),
        P("tensor", "expert"),
        P(("group", "expert"), None),
        P(),
        P(("group", "expert"), None),
        P(("group", "expert"), None),
        P(("group", "expert"), None),
        P("expert", "tensor", None),
        P("expert", "tensor", None),
        P("expert", None, "tensor"),
    )
    return jax.shard_map(
        functools.partial(body, mesh.shape["expert"], mesh.shape["tensor"]),
        mesh=mesh,
        in_specs=placed,
        out_specs=(
            P(("group", "expert"), "tensor"),
            P(("group", "expert"), "tensor"),
            P(("group", "expert")),
        ),
        check_vma=False,
    )
```

profile of v0, /device:TPU:20, one launch (start us, length us, event | category | flops | bytes accessed | tf_op | source)
XLA Modules:
  0.0 199.0 jit_solution(18417532884598780404)
XLA Ops:
  7.2 0.0 copy-start
  7.2 0.0 all-gather.2.cloned.1.call-start
  7.2 2.1 %multiply_reduce_fusion = f32[128]{0:T(128)S(1)} fusion(bf16[128,7168]{1,0:T(8,128)(2,1)} %param.16), kind=kLoop, calls=%fused_computation.4 | loop fusion | flops 2752384 | bytes 1835520 | tf_op jit(solution)/shard_map/reduce_sum | solution.py:616
  9.3 0.8 dynamic_slice.11
  10.1 2.0 multiply_convert_fusion
  12.1 0.0 all-gather.2.cloned.1.call-update
  12.1 0.9 constant_dynamic-update-slice_fusion.4
  13.0 0.7 select_reduce_fusion.1
  13.8 27.7 %all_gather.6 = bf16[512,640]{0,1:T(8,128)(2,1)S(1)} all-gather(bf16[128,640]{0,1:T(8,128)(2,1)S(1)} %constant_dynamic-update-slice_fusion), channel_id=1, replica_groups=mesh['group'=2,'expert'=4,'tensor'=4] {'expert'}, dimensions={0}, use_global_device_ids=true | all-gather | bytes 819200 | tf_op jit(solution)/shard_map/all_gather | solution.py:604
  41.6 0.2 fusion.17
  41.7 0.4 select_reduce_fusion
  42.1 1.3 copy.36.row_gate_ref
  43.4 0.1 broadcast_in_dim.66
  43.5 0.1 ge.15
  43.5 5.0 %reshape.40 = bf16[2048,576]{1,0:T(8,128)(2,1)} reshape(bf16[128,9216]{1,0:T(8,128)(2,1)} %param.12) | data formatting | bytes 4718592 | tf_op jit(solution)/shard_map/reshape | solution.py:75
  48.6 3.8 %fusion = (f32[2048]{0:T(1024)S(1)}, f32[512,2048]{1,0:T(8,128)S(1)}) fusion(s32[2048]{0:T(1024)S(1)} %ge.15, bf16[2048,576]{1,0:T(8,128)(2,1)} %reshape.40, bf16[512,640]{0,1:T(8,128)(2,1)S(1)} %all_gather.6), kind=kOutput, calls=%fused_computation.5 | convolution fusion | flops 1212151808 | bytes 7159808 | tf_op jit(solution)/shard_map/dot_general | solution.py:81
  52.4 1.2 fusion.1
  53.6 1.8 divide_convert_fusion
  55.4 0.0 copy-start.2
  55.4 0.0 copy-start.4
  55.4 0.0 copy-start.3
  55.4 2.7 %fusion.13 = bf16[16,128,128]{1,2,0:T(8,128)(2,1)S(1)} fusion(bf16[16,512,128]{2,1,0:T(8,128)(2,1)S(1)} %copy-done, bf16[128,16,512]{2,1,0:T(8,128)(2,1)S(1)} %bitcast.24), kind=kOutput, calls=%fused_computation.21 | convolution fusion | flops 268697600 | bytes 4718592 | tf_op jit(solution)/shard_map/thc,hcv->thv/dot_general | solution.py:100
  58.2 1.0 copy.38.heads_ref
  59.2 0.5 select_reduce_fusion.2
  59.8 1.1 fusion.12.picks_ref
  60.9 1.3 fusion.11.picks_t_ref
  62.2 1.3 fusion.29
  63.5 0.2 slice-done
  63.7 1.4 pad_maximum_fusion.normed_ref
  65.0 123.4 %shard_map.139 = (bf16[128,1792]{1,0:T(8,128)(2,1)}, bf16[128,1792]{1,0:T(8,128)(2,1)}) custom-call(bf16[8,192,256]{2,1,0:T(8,128)(2,1)} %fusion.12.picks_ref, bf16[8,256,192]{2,1,0:T(8,128)(2,1)} %fusion.11.picks_t_ref, f32[8,192,1]{2,1,0:T(8,128)} %copy.36.row_gate_ref, bf16[512,1792]{1,0:T(8,128)(2,1)} %pad_maximum_fusion.normed_ref, ...), custom_call_target="tpu_custom_call" | custom-call | flops 19730006016 | bytes 88080384 | tf_op jit(solution)/shard_map/pallas_call | solution.py:525
  188.5 1.8 copy.49
  190.3 1.8 copy.50
  (21 shorter events, 0.1 us)
Async XLA Ops:
  7.2 48.3 %copy-start = (bf16[16,512,128]{2,1,0:T(8,128)(2,1)S(1)}, bf16[16,512,128]{2,1,0:T(8,128)(2,1)}, u32[]{:S(2)}) copy-start(bf16[16,512,128]{2,1,0:T(8,128)(2,1)} %param.14) | copy-start | bytes 6291460
  7.2 55.0 %all-gather.2.cloned.1.call-start = ((), (), s32[]{:S(2)}) async-start(), calls=%async_computation | async-start | bytes 2293760 | tf_op jit(solution)/shard_map/all_gather | solution.py:620
  55.4 3.8 %copy-start.2 = (s32[128,8]{0,1:T(8,128)S(1)}, s32[128,8]{0,1:T(8,128)}, u32[]{:S(2)}) copy-start(s32[128,8]{0,1:T(8,128)} %param.19) | copy-start | bytes 12292
  55.4 3.8 %copy-start.4 = (s32[128,8]{0,1:T(8,128)S(1)}, s32[128,8]{0,1:T(8,128)}, u32[]{:S(2)}) copy-start(s32[128,8]{0,1:T(8,128)} %param.18) | copy-start | bytes 12292
  55.4 3.8 %copy-start.3 = (f32[128,8]{0,1:T(8,128)S(1)}, f32[128,8]{0,1:T(8,128)}, u32[]{:S(2)}) copy-start(f32[128,8]{0,1:T(8,128)} %param.20) | copy-start | bytes 12292
  62.2 1.5 slice-start
  65.0 127.1 %copy-start.1 = (bf16[16,512,128]{2,1,0:T(8,128)(2,1)S(1)}, bf16[16,512,128]{2,1,0:T(8,128)(2,1)}, u32[]{:S(2)}) copy-start(bf16[16,512,128]{2,1,0:T(8,128)(2,1)} %param.14) | copy-start | bytes 6291460
Sparse Core Ops, SparseCore 0:
  12.2 46.3 all-gather.1
where the time goes:
time: 200 us; the launch traced here: 199 us
  Pallas kernels  123 us (62%)
  blocking collectives  27.7 us (14%)
  local copies, waits for them, and re-layouts  14.3 us (7%)
  between operations  14.2 us (7%)
  other arithmetic  10.7 us (5%)
  matrix products  8.51 us (4%)
    pallas_call x1, Pallas kernels, run_fused(): pl.pallas_call(fused_kernel, out_shape=[jax.ShapeDtypeStruct(block, bf16)...  123 us
    all_gather x1, blocking collectives, body(): lax.all_gather(jnp.concatenate([kv_latent, *gate_terms], axis=1), 'expert...  27.7 us
    reshape x1, local copies, waits for them, and re-layouts, attention(): queries = q_absorbed.reshape(token_count * heads_here, key_width)  5.03 us
    unnamed x13, local copies, waits for them, and re-layouts  4.59 us
  transfers between devices with their start and end apart: 1, of which 0 were waited for; matrix products, arithmetic and copies ran while one was open for 11% of the time, Pallas kernels for 0%

commit v1 on v0

--- a/solution.py
+++ b/solution.py
@@ -308,8 +308,11 @@
 
     def multiply(s):
         slot = lax.rem(s, 2)
-        half_tokens = picks_ref.shape[2]
-        first_token = pl.multiple_of(s // local * half_tokens, half_tokens)
+        half = s // local
+        outer = pl.ds(pl.multiple_of(half * token_count, token_count), token_count)
+        inner = pl.ds(
+            pl.multiple_of((blocks - 1 - half) * token_count, token_count), token_count
+        )
 
         @pl.when(s + 1 < steps)
         def _():
@@ -319,17 +322,24 @@
         @pl.loop(0, width // tile)
         def _(j):
             cols = pl.ds(pl.multiple_of(j * tile, tile), tile)
-            rows[:, cols] = jnp.dot(
-                picks_ref[s],
-                normed_ref[pl.ds(first_token, half_tokens), cols],
-                preferred_element_type=jnp.float32,
+            rows[:, cols] = (
+                jnp.dot(
+                    picks_ref[s, :, :token_count],
+                    normed_ref[outer, cols],
+                    preferred_element_type=jnp.float32,
+                )
+                + jnp.dot(
+                    picks_ref[s, :, token_count:],
+                    normed_ref[inner, cols],
+                    preferred_element_type=jnp.float32,
+                )
             ).astype(jnp.bfloat16)
 
         for copy in weight_copies(s):
             copy.wait()
-        for half, target in ((1 - core, for_core), (core, own_half)):
+        for core_half, target in ((1 - core, for_core), (core, own_half)):
             for k, x_half in enumerate((1 - side, side)):
-                first = pl.multiple_of((half * 2 + x_half) * quarter, quarter)
+                first = pl.multiple_of((core_half * 2 + x_half) * quarter, quarter)
                 cols = pl.ds(first, quarter)
                 for m, buf in enumerate((gate_buf, up_buf)):
                     target[slot, 2 * k + m] = jnp.dot(
@@ -467,30 +477,30 @@
         def _():
             pass_on(step - 3)
 
+        @pl.when(step == steps - 2)
+        def _():
+            add_cols_core()
+
+        @pl.when(step == steps - 1)
+        def _():
+            add_cols_x()
+
         @pl.when(step >= 4)
         def _():
             project(step - 4)
 
-        @pl.when(step == steps - 2)
+        @pl.when(step == steps - 3)
         def _():
             multiply_heads()
-
-        @pl.when(step == steps - 1)
-        def _():
-            add_cols_core()
-
-        @pl.when(step == steps)
-        def _():
-            add_cols_x()
 
     @pl.when(jnp.logical_not(stays))
     def _():
         cols_final_copy().wait()
-        attended_ref[...] = cols_in[...]
+        attended_ref[...] = cols_in[...].astype(jnp.float32)
 
     @pl.when(stays)
     def _():
-        attended_ref[...] = cols_out[...]
+        attended_ref[...] = cols_out[...].astype(jnp.float32)
 
     for half in range(2):
         for i in range(2):
@@ -508,7 +518,7 @@
     mixed = mix_in[0].astype(jnp.float32)
     for source in range(1, blocks):
         mixed += mix_in[source].astype(jnp.float32)
-    mixture_ref[...] = mixed.astype(jnp.bfloat16)
+    mixture_ref[...] = mixed
 
 
 def run_fused(picks, picks_t, row_gate, normed_all, heads_out, w_gate, w_up, w_down, w_out):
@@ -524,7 +534,7 @@
     block = (token_count, width)
     return pl.pallas_call(
         fused_kernel,
-        out_shape=[jax.ShapeDtypeStruct(block, bf16)] * 2,
+        out_shape=[jax.ShapeDtypeStruct(block, f32)] * 2,
         in_specs=[vmem] * 5 + [hbm] * 4,
         out_specs=[vmem] * 2,
         scratch_shapes=[
@@ -601,9 +611,18 @@
         rest = rest - term
     fill = -(kv_latent.shape[1] + 3 * experts) % 128
     gate_terms.append(jnp.zeros((gate_map.shape[0], fill), jnp.bfloat16))
-    mixed = lax.all_gather(
-        jnp.concatenate([kv_latent, *gate_terms], axis=1), "expert", axis=0, tiled=True
-    )
+    mixed = jnp.concatenate([kv_latent, *gate_terms], axis=1)
+    if n_tensor % 2 == 0:
+        own = lax.axis_index("tensor") & 1
+        half_rows = mixed.shape[0] // 2
+        part = lax.dynamic_slice_in_dim(mixed, own * half_rows, half_rows, 0)
+        part = lax.all_gather(part, "expert", axis=0, tiled=False)
+        got = lax.ppermute(part, "tensor", [(i, i ^ 1) for i in range(n_tensor)])
+        mixed = jnp.concatenate(
+            [jnp.where(own == 0, part, got), jnp.where(own == 0, got, part)], axis=1
+        ).reshape(-1, mixed.shape[1])
+    else:
+        mixed = lax.all_gather(mixed, "expert", axis=0, tiled=True)
     key_width = kv_latent.shape[1]
     kv_all = mixed[:, :key_width]
     gate_all = sum(
@@ -626,25 +645,24 @@
     )
     if n_tensor == 4 and n_expert == 4 and hidden % 1024 == 0 and slice_width % 256 == 0:
         block = tokens // 4
-        halves = [
-            jnp.concatenate([part[:block], part[3 * block :], part[block : 3 * block]], axis=0)
-            for part in (gate_here, normed_all)
-        ]
-        gate_halves = halves[0].reshape(2, 2 * block, local).transpose(0, 2, 1)
+        gate_halves = jnp.concatenate(
+            [gate_here[:block], gate_here[3 * block :], gate_here[block : 3 * block]], axis=0
+        )
+        gate_halves = gate_halves.reshape(2, 2 * block, local).transpose(0, 2, 1)
         depth = -(-2 * (CAP + CAP_C) // 16) * 16
         picks, row_gate = place_rows(gate_halves.reshape(2 * local, 2 * block), depth)
         attended, mixture = run_fused(
             picks,
             picks.transpose(0, 2, 1),
             row_gate[:, :, None],
-            halves[1],
+            normed_all,
             heads_out,
             w_gate,
             w_up,
             w_down,
             w_out,
         )
-        return (attended, mixture, missed)
+        return (attended.astype(jnp.bfloat16), mixture.astype(jnp.bfloat16), missed)
 
     depth = n_expert * (CAP + CAP_C)
     picks, row_gate = place_rows(gate_here.T, depth)

time: 200 us -> 214 us (1.070)
  waiting for transfers between devices: 0.02 us -> 22.8 us
  blocking collectives: 27.7 us -> 12.4 us
  Pallas kernels: 123 us -> 131 us
  local copies, waits for them, and re-layouts: 14.3 us -> 10.6 us
  other arithmetic: 10.7 us -> 13.5 us
    all_gather x1, waiting for transfers between devices: 0.01 us -> 22.8 us  [body(): normed_all = lax.all_gather(normed, 'expert', axis=0, tiled=True)]
    all_gather x1, blocking collectives: 27.7 us -> 12.4 us  [body(): part = lax.all_gather(part, 'expert', axis=0, tiled=False)]
    pallas_call x1, Pallas kernels: 123 us -> 131 us  [run_fused(): pl.pallas_call(fused_kernel, out_shape=[jax.ShapeDtypeStruct(block, f32)]...]
    convert_element_type x0 -> x3, other arithmetic: none -> 4 us  [the longest x2 3.99 us: body(): return (attended.astype(jnp.bfloat16), mixture.astype(jnp.bfloat16), missed)]
    unnamed x13 -> x14, local copies, waits for them, and re-layouts: 4.59 us -> 1.41 us
  transfers between devices with their start and end apart: 1 -> 2, of which waited for: 0 -> 1; matrix products, arithmetic and copies ran while one was open for 11% -> 12% of each run, Pallas kernels for 0% -> 0%
where the time goes in v1:
time: 214 us; the launch traced here: 213 us
  Pallas kernels  131 us (61%)
  waiting for transfers between devices  22.8 us (11%)
  between operations  14.2 us (7%)
  other arithmetic  13.5 us (6%)
  blocking collectives  12.4 us (6%)
  local copies, waits for them, and re-layouts  10.6 us (5%)
  matrix products  8.27 us (4%)
    pallas_call x1, Pallas kernels, run_fused(): pl.pallas_call(fused_kernel, out_shape=[jax.ShapeDtypeStruct(block, f32)]...  131 us
    all_gather x1, waiting for transfers between devices, body(): normed_all = lax.all_gather(normed, 'expert', axis=0, tiled=True)  22.8 us
    all_gather x1, blocking collectives, body(): part = lax.all_gather(part, 'expert', axis=0, tiled=False)  12.4 us
    reshape x1, local copies, waits for them, and re-layouts, attention(): queries = q_absorbed.reshape(token_count * heads_here, key_width)  5.01 us
  transfers between devices with their start and end apart: 2, of which 1 were waited for; matrix products, arithmetic and copies ran while one was open for 12% of the time, Pallas kernels for 0%

profile of v1, /device:TPU:20, one launch (start us, length us, event | category | flops | bytes accessed | tf_op | source)
XLA Modules:
  0.0 213.3 jit_solution(1168291820895552218)
XLA Ops:
  7.2 0.9 select_reduce_fusion.1
  8.1 0.1 copy.44
  8.2 0.1 copy.45
  8.3 0.1 copy.46
  8.5 1.1 copy.43
  9.6 0.1 concatenate.9
  9.7 12.4 %all-gather = bf16[256,640]{1,0:T(8,128)(2,1)S(1)} all-gather(bf16[64,640]{1,0:T(8,128)(2,1)S(1)} %constant_dynamic-slice_fusion.3), channel_id=2, replica_groups=mesh['group'=2,'expert'=4,'tensor'=4] {'expert'}, dimensions={0}, use_global_device_ids=true | all-gather | bytes 409600 | tf_op jit(solution)/shard_map/all_gather | solution.py:619
  22.1 2.0 multiply_reduce_fusion
  24.1 0.8 dynamic_slice.15
  24.9 2.0 multiply_convert_fusion
  27.1 5.0 %reshape.44 = bf16[2048,576]{1,0:T(8,128)(2,1)} reshape(bf16[128,9216]{1,0:T(8,128)(2,1)} %param.12) | data formatting | bytes 4718592 | tf_op jit(solution)/shard_map/reshape | solution.py:75
  32.1 0.5 select_reduce_fusion.2
  32.8 3.7 %fusion = (f32[2048]{0:T(1024)S(1)}, f32[512,2048]{1,0:T(8,128)S(1)}) fusion(s32[2048]{0:T(1024)S(1)} %ge.15, bf16[2048,576]{1,0:T(8,128)(2,1)} %reshape.44, bf16[512,640]{1,0:T(8,128)(2,1)S(1)} %bitcast.23), kind=kOutput, calls=%fused_computation.5 | convolution fusion | flops 1212151808 | bytes 7225344 | tf_op jit(solution)/shard_map/dot_general | solution.py:81
  36.5 1.2 fusion.1
  37.7 1.7 divide_convert_fusion
  39.4 2.7 %fusion.13 = bf16[16,128,128]{1,2,0:T(8,128)(2,1)S(1)} fusion(bf16[16,512,128]{2,1,0:T(8,128)(2,1)S(1)} %copy-done, bf16[128,16,512]{2,1,0:T(8,128)(2,1)S(1)} %bitcast.31), kind=kOutput, calls=%fused_computation.20 | convolution fusion | flops 268697600 | bytes 4718592 | tf_op jit(solution)/shard_map/thc,hcv->thv/dot_general | solution.py:100
  42.1 1.0 copy.55.heads_ref
  43.1 0.2 fusion.29
  43.3 0.1 constant_dynamic-slice_fusion
  43.5 0.1 copy.59
  43.6 0.1 copy.60
  43.7 0.1 constant_dynamic-slice_fusion.2
  43.8 0.1 copy.61
  44.0 0.2 fusion.17
  44.1 0.4 select_reduce_fusion
  44.5 1.3 copy.53.row_gate_ref
  45.8 1.1 fusion.12.picks_ref
  46.9 1.3 fusion.11.picks_t_ref
  48.2 22.8 %all-gather.3.cloned.1.call-done.normed_ref = bf16[512,1792]{1,0:T(8,128)(2,1)} async-done(((bf16[128,1792]{1,0:T(8,128)(2,1)}), bf16[512,1792]{1,0:T(8,128)(2,1)}) %all-gather.3.cloned.1.call-update) | async-done | bytes 1835024 | tf_op jit(solution)/shard_map/all_gather | solution.py:639
  71.0 131.5 %shard_map.139 = (f32[128,1792]{1,0:T(8,128)}, f32[128,1792]{1,0:T(8,128)}) custom-call(bf16[8,192,256]{2,1,0:T(8,128)(2,1)} %fusion.12.picks_ref, bf16[8,256,192]{2,1,0:T(8,128)(2,1)} %fusion.11.picks_t_ref, f32[8,192,1]{2,1,0:T(8,128)} %copy.53.row_gate_ref, bf16[512,1792]{1,0:T(8,128)(2,1)} %all-gather.3.cloned.1.call-done.normed_ref, ...), custom_call_target="tpu_custom_call" | custom-call | flops 19730006016 | bytes 88080384 | tf_op jit(solution)/shard_map/pallas_call | solution.py:535
  202.5 2.0 convert_element_type.71
  204.5 2.0 convert_element_type.72
  (29 shorter events, 0.5 us)
Async XLA Ops:
  7.2 32.2 %copy-start = (bf16[16,512,128]{2,1,0:T(8,128)(2,1)S(1)}, bf16[16,512,128]{2,1,0:T(8,128)(2,1)}, u32[]{:S(2)}) copy-start(bf16[16,512,128]{2,1,0:T(8,128)(2,1)} %param.14) | copy-start | bytes 6291460
  7.2 63.8 %all-gather.3.cloned.1.call-start = ((), (), s32[]{:S(2)}) async-start(), calls=%async_computation | async-start | bytes 2293760 | tf_op jit(solution)/shard_map/all_gather | solution.py:639
  22.1 10.5 %collective-permute-start = (bf16[4,64,640]{2,1,0:T(8,128)(2,1)S(1)}, bf16[4,64,640]{2,1,0:T(8,128)(2,1)S(1)}, u32[]{:S(2)}, u32[]{:S(2)}) collective-permute-start(bf16[4,64,640]{2,1,0:T(8,128)(2,1)S(1)} %bitcast.26), channel_id=1, source_target_pairs={{0,1},{1,0},{2,3},{3,2},{4,5},{5,4},{6,7},{7,6},{8,9},{9,8},{10,11... | collective-permute-start | bytes 983048 | tf_op jit(solution)/shard_map/ppermute | solution.py:620
  22.1 10.0 %copy-start.2 = (s32[128,8]{0,1:T(8,128)S(1)}, s32[128,8]{0,1:T(8,128)}, u32[]{:S(2)}) copy-start(s32[128,8]{0,1:T(8,128)} %param.19) | copy-start | bytes 12292
  22.1 10.0 %copy-start.4 = (s32[128,8]{0,1:T(8,128)S(1)}, s32[128,8]{0,1:T(8,128)}, u32[]{:S(2)}) copy-start(s32[128,8]{0,1:T(8,128)} %param.18) | copy-start | bytes 12292
  22.1 10.0 %copy-start.3 = (f32[128,8]{0,1:T(8,128)S(1)}, f32[128,8]{0,1:T(8,128)}, u32[]{:S(2)}) copy-start(f32[128,8]{0,1:T(8,128)} %param.20) | copy-start | bytes 12292
  71.0 135.5 %copy-start.1 = (bf16[16,512,128]{2,1,0:T(8,128)(2,1)S(1)}, bf16[16,512,128]{2,1,0:T(8,128)(2,1)}, u32[]{:S(2)}) copy-start(bf16[16,512,128]{2,1,0:T(8,128)(2,1)} %param.14) | copy-start | bytes 6291460
Sparse Core Ops, SparseCore 0:
  27.0 43.9 all-gather.2
